TPU v7x, 32 devices: a whole 2x2x4 slice. The times are simulated.
32 devices in a mesh: dp: 8 (over y, x, core), cent: 4 (over z).
Axes of the slice: x: 2, y: 2, z: 4, core: 2. Of those that a mesh axis runs over, the one named last changes fastest.
Arguments:
- embeddings: bfloat16 [8192, 768], P(('dp', 'cent')), may hold values from -6 to 6
- centroids: bfloat16 [2048, 768], P('cent'), may hold values from -6 to 6
- assign: int32 [8192], P(('dp', 'cent')), may hold values from 0 to 2047, as said below
- bins: int32 [8192], P(('dp', 'cent')), may hold values from 0 to 255
Outputs:
- quant_error: float32 [8192], P(('dp', 'cent'))
- new_centroids: float32 [2048, 768], P(('cent', 'dp'))
- histograms: float32 [2048, 256], P(('cent', 'dp'))
Inputs may be any that keep to these rules, and one draw needn't show every extreme that they name: `assign`: list k belongs to owner k // 64; among the 256 rows of one device (aligned blocks) at most 16 name lists of any one owner.
All inputs are finite; a program needn't handle non-finite values.
Results may differ from a plain program's by a relative error of at most 0.0003.
Values may be sent and summed in bfloat16 or wider, within the bound.
A program may use at most 128 MiB of HBM per device.

v0:
```python
import jax
import jax.numpy as jnp
from jax import lax
from jax.sharding import PartitionSpec as P

LISTS_DEV = 64
NBINS = 256


epsilon = 1e-06


def per_device(embeddings, centroids, assign, bins):
    row_count, feature_dim = embeddings.shape
    row_f32 = embeddings.astype(jnp.float32)
    row_sq = jnp.sum(row_f32 * row_f32, axis=1)
    start_sq = jnp.full((row_count,), 3e38, jnp.float32)
    block_rows = lax.all_gather(centroids, "cent", axis=0, tiled=True)
    products = jnp.einsum("rd,kd->rk", embeddings, block_rows, preferred_element_type=jnp.float32)
    block_f32 = block_rows.astype(jnp.float32)
    cent_sq = jnp.sum(block_f32 * block_f32, axis=1)
    nearest_sq = jnp.minimum(start_sq, jnp.min(cent_sq[None, :] - 2.0 * products, axis=1))
    quant_error = (nearest_sq + row_sq) / feature_dim
    dp_count = lax.axis_size("dp")
    cent_count = lax.axis_size("cent")
    owner_count = dp_count * cent_count
    slot_cap = 2 * row_count // owner_count
    owner_id = assign // LISTS_DEV
    local_list = assign % LISTS_DEV
    dest_slot = owner_id % dp_count * cent_count + owner_id // dp_count
    owner_hits = (dest_slot[:, None] == jnp.arange(owner_count, dtype=jnp.int32)[None, :]).astype(
        jnp.int32
    )
    earlier = jnp.cumsum(owner_hits, axis=0) - owner_hits
    slot_id = jnp.sum(earlier * owner_hits, axis=1)
    position = dest_slot * slot_cap + slot_id
    outgoing = (
        jnp.zeros((owner_count * slot_cap, feature_dim), jnp.bfloat16).at[position].set(embeddings)
    )
    outgoing = outgoing.reshape(dp_count, cent_count, slot_cap, feature_dim)
    tag_values = jnp.stack([local_list, bins], axis=1).astype(jnp.float32)
    labels = jnp.full((owner_count * slot_cap, 2), -1.0, jnp.float32).at[position].set(tag_values)
    labels = labels.astype(jnp.bfloat16).reshape(dp_count, cent_count, slot_cap, 2)
    arrived, arrived_tags = (
        lax.all_to_all(
            lax.all_to_all(outgoing, "dp", split_axis=0, concat_axis=0, tiled=True),
            "cent",
            split_axis=1,
            concat_axis=1,
            tiled=True,
        ),
        lax.all_to_all(
            lax.all_to_all(labels, "dp", split_axis=0, concat_axis=0, tiled=True),
            "cent",
            split_axis=1,
            concat_axis=1,
            tiled=True,
        ),
    )
    arrived = arrived.reshape(-1, feature_dim).astype(jnp.float32)
    arrived_tags = arrived_tags.reshape(-1, 2).astype(jnp.int32)
    list_ids = arrived_tags[:, 0]
    bin_ids = arrived_tags[:, 1]
    member = (list_ids[:, None] == jnp.arange(LISTS_DEV, dtype=jnp.int32)[None, :]).astype(
        jnp.float32
    )
    own_rows = lax.dynamic_slice_in_dim(
        centroids, lax.axis_index("dp") * LISTS_DEV, LISTS_DEV, 0
    ).astype(jnp.float32)
    highest = lax.Precision.HIGHEST
    residual = arrived - jnp.dot(member, own_rows, precision=highest)
    residual_sums = jnp.dot(member.T, residual, precision=highest)
    counts = jnp.sum(member, axis=0)
    updated = own_rows + residual_sums / jnp.maximum(counts, 1.0)[:, None]
    residual_norm = jnp.sqrt(jnp.mean(residual * residual, axis=1) + epsilon)
    bin_hits = (bin_ids[:, None] == jnp.arange(NBINS, dtype=jnp.int32)[None, :]).astype(jnp.float32)
    histogram = jnp.dot(member.T, bin_hits * residual_norm[:, None], precision=highest)
    return (quant_error, updated, histogram)


def solution(mesh):
    in_specs = (P(("dp", "cent"), None), P("cent", None), P(("dp", "cent")), P(("dp", "cent")))
    out_specs = (P(("dp", "cent")), P(("cent", "dp"), None), P(("cent", "dp"), None))
    return jax.shard_map(
        per_device, mesh=mesh, in_specs=in_specs, out_specs=out_specs, check_vma=False
    )
```

profile of v0, /device:TPU:0, one launch (start us, length us, event | category | flops | bytes accessed | tf_op | source)
XLA Modules:
  0.0 106.1 jit_solution(10800557101772743024)
XLA Ops:
  7.2 0.0 all-gather.2.cloned.1.call-start
  7.2 0.7 all-gather.2.cloned.1.call-update
  7.9 0.7 and_select_fusion
  8.6 0.6 reduce-window.6
  9.2 0.2 slice_reduce_fusion
  9.4 0.7 add_convert_fusion
  10.1 0.1 copy.32
  10.3 0.1 fusion.18
  10.4 1.2 %scatter_custom_fusion = f32[512,2]{1,0:T(8,128)S(1)} fusion(s32[256]{0:T(256)S(1)} %compare_select_fusion, f32[256,2]{1,0:T(8,128)S(1)} %copy.32, f32[]{:T(128)} %constant.76.clone.1), kind=kCustom, calls=%fused_computation.21 | custom fusion | bytes 4100 | tf_op jit(solution)/shard_map/scatter | solution.py:42
  11.6 0.9 copy.33
  12.5 5.2 %all-to-all-start = ((bf16[8,4,16,2]{2,1,3,0:T(4,128)(2,1)}), bf16[8,4,16,2]{2,1,3,0:T(4,128)(2,1)S(1)}, u32[]{:S(2)}, u32[]{:S(2)}) async-start(bf16[8,4,16,2]{2,1,3,0:T(4,128)(2,1)} %copy.33), calls=%async_computation | async-start | bytes 32768 | tf_op jit(solution)/shard_map/all_to_all | solution.py:53
  17.7 3.1 %scatter_custom_fusion.1 = bf16[512,768]{1,0:T(8,128)(2,1)} fusion(s32[256]{0:T(256)S(1)} %compare_select_fusion, bf16[256,768]{1,0:T(8,128)(2,1)} %param.4, bf16[]{:T(256)} %constant.86.clone.1), kind=kCustom, calls=%fused_computation.14 | custom fusion | bytes 786944 | tf_op jit(solution)/shard_map/scatter | solution.py:38
  20.7 1.7 %all-to-all-done = bf16[8,4,16,2]{2,1,3,0:T(4,128)(2,1)S(1)} async-done(((bf16[8,4,16,2]{2,1,3,0:T(4,128)(2,1)}), bf16[8,4,16,2]{2,1,3,0:T(4,128)(2,1)S(1)}, u32[]{:S(2)}, u32[]{:S(2)}) %all-to-all-start) | async-done | bytes 2080 | tf_op jit(solution)/shard_map/all_to_all | solution.py:53
  22.4 0.0 copy-start.1
  22.4 3.7 %all-to-all-start.2 = ((bf16[8,4,16,768]{3,2,1,0:T(8,128)(2,1)}), bf16[8,4,16,768]{3,2,1,0:T(8,128)(2,1)S(1)}, u32[]{:S(2)}, u32[]{:S(2)}) async-start(bf16[8,4,16,768]{3,2,1,0:T(8,128)(2,1)} %bitcast.6), calls=%async_computation.2 | async-start | bytes 1572864 | tf_op jit(solution)/shard_map/all_to_all | solution.py:46
  26.1 0.7 reshape.71
  26.8 11.8 %all-to-all-done.2 = bf16[8,4,16,768]{3,2,1,0:T(8,128)(2,1)S(1)} async-done(((bf16[8,4,16,768]{3,2,1,0:T(8,128)(2,1)}), bf16[8,4,16,768]{3,2,1,0:T(8,128)(2,1)S(1)}, u32[]{:S(2)}, u32[]{:S(2)}) %all-to-all-start.2) | async-done | bytes 786464 | tf_op jit(solution)/shard_map/all_to_all | solution.py:46
  38.7 4.9 %all-to-all-start.1 = ((bf16[4,2,128]{2,1,0:T(2,128)(2,1)}), bf16[4,2,128]{2,1,0:T(2,128)(2,1)S(1)}, u32[]{:S(2)}, u32[]{:S(2)}) async-start(bf16[4,2,128]{2,1,0:T(2,128)(2,1)} %reshape.71), calls=%async_computation.1 | async-start | bytes 4096 | tf_op jit(solution)/shard_map/all_to_all | solution.py:52
  43.5 0.9 copy.36
  44.5 4.6 %all-to-all-done.1 = bf16[4,2,128]{2,1,0:T(2,128)(2,1)S(1)} async-done(((bf16[4,2,128]{2,1,0:T(2,128)(2,1)}), bf16[4,2,128]{2,1,0:T(2,128)(2,1)S(1)}, u32[]{:S(2)}, u32[]{:S(2)}) %all-to-all-start.1) | async-done | bytes 2080 | tf_op jit(solution)/shard_map/all_to_all | solution.py:52
  49.1 3.5 %all-to-all-start.3 = ((bf16[8,4,16,768]{3,2,0,1:T(8,128)(2,1)}), bf16[8,4,16,768]{3,2,0,1:T(8,128)(2,1)S(1)}, u32[]{:S(2)}, u32[]{:S(2)}) async-start(bf16[8,4,16,768]{3,2,0,1:T(8,128)(2,1)} %copy.36), calls=%async_computation.3 | async-start | bytes 1572864 | tf_op jit(solution)/shard_map/all_to_all | solution.py:45
  52.6 0.0 copy-done.1
  52.6 0.2 multiply_reduce_fusion.2
  52.8 0.1 reshape.72
  52.9 0.1 reshape.46
  53.0 0.1 convert_reduce_fusion
  53.1 36.6 %all-to-all-done.3 = bf16[8,4,16,768]{3,2,0,1:T(8,128)(2,1)S(1)} async-done(((bf16[8,4,16,768]{3,2,0,1:T(8,128)(2,1)}), bf16[8,4,16,768]{3,2,0,1:T(8,128)(2,1)S(1)}, u32[]{:S(2)}, u32[]{:S(2)}) %all-to-all-start.3) | async-done | bytes 786464 | tf_op jit(solution)/shard_map/all_to_all | solution.py:45
  89.8 0.2 copy.37
  89.9 1.4 %multiply_reduce_fusion.1 = (f32[512]{0:T(512)S(1)}, f32[512,768]{1,0:T(8,128)S(1)}) fusion(bf16[512,768]{1,0:T(8,128)(2,1)} %param.5, s32[]{:T(128)S(6)} %select_n.26, s32[512]{0:T(512)S(1)} %bitcast.41, f32[8,4,16,768]{3,2,1,0:T(8,128)S(1)} %copy.37), kind=kOutput, calls=%fused_computation.6 | convolution fusion | flops 51543552 | bytes 3248132 | tf_op jit(solution)/shard_map/dot_general | solution.py:71
  91.4 1.1 %fusion.3 = f32[64,256]{1,0:T(8,128)} fusion(f32[512]{0:T(512)S(1)} %add_sqrt_fusion, s32[512]{0:T(512)S(1)} %bitcast.46, s32[512]{0:T(512)S(1)} %bitcast.42), kind=kOutput, calls=%fused_computation.11 | convolution fusion | flops 100958208 | bytes 71680 | tf_op jit(solution)/shard_map/dot_general | solution.py:77
  92.4 2.3 %fusion.2 = f32[64,768]{1,0:T(8,128)} fusion(f32[512,768]{1,0:T(8,128)S(1)} %get-tuple-element.8, f32[64]{0:T(128)S(1)} %broadcast_maximum_fusion, bf16[512,768]{1,0:T(8,128)(2,1)} %param.5, s32[]{:T(128)S(6)} %select_n.26, s32[512]{0:T(512)S(1)} %bitcast.43), kind=kOutput, calls=%fused_computation.9 | convolution fusion | flops 302170112 | bytes 1870084 | tf_op jit(solution)/shard_map/dot_general | solution.py:72
  94.7 0.0 all-gather.2.cloned.1.call-done
  94.7 0.0 copy-start
  94.7 2.7 %multiply_reduce_fusion = f32[2048]{0:T(1024)S(1)} fusion(bf16[2048,768]{1,0:T(8,128)(2,1)} %all-gather.2.cloned.1.call-done), kind=kLoop, calls=%fused_computation.2 | loop fusion | flops 4716544 | bytes 3153920 | tf_op jit(solution)/shard_map/reduce_sum | solution.py:21
  97.5 0.1 copy-done
  97.6 1.1 %fusion.1 = f32[256]{0:T(256)S(1)} fusion(bf16[256,768]{1,0:T(8,128)(2,1)S(1)} %copy-done.1, bf16[2048,768]{1,0:T(8,128)(2,1)S(1)} %copy-done, f32[2048]{0:T(1024)S(1)} %multiply_reduce_fusion), kind=kOutput, calls=%fused_computation.7 | convolution fusion | flops 806878976 | bytes 3548160 | tf_op jit(solution)/shard_map/rd,kd->rk/dot_general | solution.py:19
  98.7 0.6 add_multiply_fusion
  (11 shorter events, 0.1 us)
Async XLA Ops:
  7.2 87.6 %all-gather.2.cloned.1.call-start = ((), (), s32[]{:S(2)}) async-start(), calls=%async_computation.4 | async-start | bytes 3932160 | tf_op jit(solution)/shard_map/all_gather | solution.py:18
  12.5 9.9 %all-to-all-start = ((bf16[8,4,16,2]{2,1,3,0:T(4,128)(2,1)}), bf16[8,4,16,2]{2,1,3,0:T(4,128)(2,1)S(1)}, u32[]{:S(2)}, u32[]{:S(2)}) async-start(bf16[8,4,16,2]{2,1,3,0:T(4,128)(2,1)} %copy.33), calls=%async_computation | async-start | bytes 32768 | tf_op jit(solution)/shard_map/all_to_all | solution.py:53
  22.4 30.2 %copy-start.1 = (bf16[256,768]{1,0:T(8,128)(2,1)S(1)}, bf16[256,768]{1,0:T(8,128)(2,1)}, u32[]{:S(2)}) copy-start(bf16[256,768]{1,0:T(8,128)(2,1)} %param.4) | copy-start | bytes 1179652
  22.4 16.2 %all-to-all-start.2 = ((bf16[8,4,16,768]{3,2,1,0:T(8,128)(2,1)}), bf16[8,4,16,768]{3,2,1,0:T(8,128)(2,1)S(1)}, u32[]{:S(2)}, u32[]{:S(2)}) async-start(bf16[8,4,16,768]{3,2,1,0:T(8,128)(2,1)} %bitcast.6), calls=%async_computation.2 | async-start | bytes 1572864 | tf_op jit(solution)/shard_map/all_to_all | solution.py:46
  38.7 10.4 %all-to-all-start.1 = ((bf16[4,2,128]{2,1,0:T(2,128)(2,1)}), bf16[4,2,128]{2,1,0:T(2,128)(2,1)S(1)}, u32[]{:S(2)}, u32[]{:S(2)}) async-start(bf16[4,2,128]{2,1,0:T(2,128)(2,1)} %reshape.71), calls=%async_computation.1 | async-start | bytes 4096 | tf_op jit(solution)/shard_map/all_to_all | solution.py:52
  49.1 40.7 %all-to-all-start.3 = ((bf16[8,4,16,768]{3,2,0,1:T(8,128)(2,1)}), bf16[8,4,16,768]{3,2,0,1:T(8,128)(2,1)S(1)}, u32[]{:S(2)}, u32[]{:S(2)}) async-start(bf16[8,4,16,768]{3,2,0,1:T(8,128)(2,1)} %copy.36), calls=%async_computation.3 | async-start | bytes 1572864 | tf_op jit(solution)/shard_map/all_to_all | solution.py:45
  94.7 2.8 %copy-start = (bf16[2048,768]{1,0:T(8,128)(2,1)S(1)}, bf16[2048,768]{1,0:T(8,128)(2,1)}, u32[]{:S(2)}) copy-start(bf16[2048,768]{1,0:T(8,128)(2,1)} %all-gather.2.cloned.1.call-done) | copy-start | bytes 9437188
Sparse Core Ops, SparseCore 0:
  9.6 82.8 all-gather.1
where the time goes:
time: 107 us; the launch traced here: 106 us
  waiting for transfers between devices  55.5 us (52%)
  starting transfers between devices  17.3 us (16%)
  between operations  14.1 us (13%)
  local copies, waits for them, and re-layouts  7.58 us (7%)
  matrix products  5.88 us (5%)
  other arithmetic  5.75 us (5%)
    all_to_all x1, waiting for transfers between devices, per_device(): lax.all_to_all(lax.all_to_all(outgoing, 'dp', split_axis=0, concat_axis=0...  36.6 us
    all_to_all x1, waiting for transfers between devices, per_device(): lax.all_to_all(outgoing, 'dp', split_axis=0, concat_axis=0, tiled=True)  11.8 us
    all_to_all x1, starting transfers between devices, per_device(): lax.all_to_all(labels, 'dp', split_axis=0, concat_axis=0, tiled=True)  5.17 us
    all_to_all x1, starting transfers between devices, per_device(): lax.all_to_all(lax.all_to_all(labels, 'dp', split_axis=0, concat_axis=0,...  4.87 us
    all_to_all x1, waiting for transfers between devices, per_device(): lax.all_to_all(lax.all_to_all(labels, 'dp', split_axis=0, concat_axis=0,...  4.63 us
    all_to_all x1, starting transfers between devices, per_device(): lax.all_to_all(outgoing, 'dp', split_axis=0, concat_axis=0, tiled=True)  3.68 us
    all_to_all x1, starting transfers between devices, per_device(): lax.all_to_all(lax.all_to_all(outgoing, 'dp', split_axis=0, concat_axis=0...  3.5 us
    scatter x1, local copies, waits for them, and re-layouts, per_device(): jnp.zeros((owner_count * slot_cap, feature_dim), jnp.bfloat16).at[position]  3.06 us
  transfers between devices with their start and end apart: 5, of which 4 were waited for; matrix products, arithmetic and copies ran while one was open for 14% of the time, Pallas kernels for 0%

commit v1 on v0

v1 whole, which is shorter than its diff:
```python
import functools

import jax
import jax.numpy as jnp
from jax import lax
from jax.experimental import pallas as pl
from jax.experimental.pallas import tpu as pltpu
from jax.sharding import PartitionSpec as P

LISTS_DEV = 64
NBINS = 256
TAGS = 128

epsilon = 1e-06
MESH = pl.DeviceIdType.MESH
NT = (((1,), (1,)), ((), ()))


def kernel(
    n_dp, n_cent, cap,
    emb_ref, cent_ref, assign_ref, bins_ref,
    quant_ref, new_ref, hist_ref,
    outbuf, inbuf, mate_rows, pieces, min_out, min_in,
    row_send, row_recv, mate_send, mate_recv, z_send, z_recv, p_send, p_recv, m_send, m_recv,
):
    rows, dim = emb_ref.shape
    lists = cent_ref.shape[0] // n_dp
    chips = n_dp // 2
    owners = n_dp * n_cent
    slots = owners * cap
    dp, ce = lax.axis_index("dp"), lax.axis_index("cent")
    chip, core = dp // 2, dp % 2
    mate = chip * 2 + (1 - core)
    me = ce * n_dp + dp

    barrier = pltpu.get_barrier_semaphore()

    def greet(i, _):
        other = lax.rem(me + i, owners)
        pl.semaphore_signal(barrier, inc=1, device_id=(other % n_dp, other // n_dp), device_id_type=MESH)
        return 0

    lax.fori_loop(1, owners, greet, 0)

    shift = lists.bit_length() - 1
    assign = assign_ref[...]
    owner = lax.shift_right_logical(assign, shift)
    local = assign - lax.shift_left(owner, shift)
    hits = lax.broadcasted_iota(jnp.int32, (owners, rows), 0) == owner
    hits_f = hits.astype(jnp.float32)
    before = lax.broadcasted_iota(jnp.int32, (rows, rows), 0) < lax.broadcasted_iota(jnp.int32, (rows, rows), 1)
    earlier = jnp.dot(
        hits_f.astype(jnp.bfloat16),
        before.astype(jnp.float32).astype(jnp.bfloat16),
        preferred_element_type=jnp.float32,
    )
    place = jnp.sum(earlier * hits_f, axis=0, keepdims=True)
    position = owner * cap + place.astype(jnp.int32)
    pick = (lax.broadcasted_iota(jnp.int32, (slots, rows), 0) == position).astype(jnp.float32).astype(jnp.bfloat16)
    tag_row = lax.broadcasted_iota(jnp.int32, (TAGS, rows), 0)
    tags = jnp.where(
        tag_row == 0,
        jnp.broadcast_to(local + 1, (TAGS, rows)),
        jnp.where(tag_row == 1, jnp.broadcast_to(bins_ref[...], (TAGS, rows)), 0),
    ).astype(jnp.float32).astype(jnp.bfloat16)
    outbuf[:, :, :dim] = (
        jnp.dot(pick, emb_ref[...], preferred_element_type=jnp.float32)
        .astype(jnp.bfloat16).reshape(owners, cap, dim)
    )
    outbuf[:, :, dim:] = (
        lax.dot_general(pick, tags, NT, preferred_element_type=jnp.float32)
        .astype(jnp.bfloat16).reshape(owners, cap, TAGS)
    )

    pl.semaphore_wait(barrier, owners - 1)

    def z_copy(i):
        other = lax.rem(ce + i, n_cent)
        return pltpu.make_async_remote_copy(
            src_ref=cent_ref.at[pl.ds(pl.multiple_of(dp * lists, lists), lists)],
            dst_ref=pieces.at[chip, ce],
            send_sem=z_send.at[other],
            recv_sem=z_recv.at[ce],
            device_id=(dp, other),
            device_id_type=MESH,
        )

    for i in range(1, n_cent):
        z_copy(i).start()
    mate_copy = pltpu.make_async_remote_copy(
        src_ref=emb_ref, dst_ref=mate_rows, send_sem=mate_send, recv_sem=mate_recv,
        device_id=(mate, ce), device_id_type=MESH,
    )
    mate_copy.start()

    def row_copy(other):
        return pltpu.make_async_remote_copy(
            src_ref=outbuf.at[other],
            dst_ref=inbuf.at[me],
            send_sem=row_send.at[other],
            recv_sem=row_recv.at[me],
            device_id=(other % n_dp, other // n_dp),
            device_id_type=MESH,
        )

    def send_rows(i, _):
        gap = i // n_dp + 1
        other = lax.rem(ce + gap, n_cent) * n_dp + lax.rem(dp + i, n_dp)
        row_copy(other).start()
        return 0

    lax.fori_loop(0, owners - n_dp, send_rows, 0)

    def send_plane(i, _):
        row_copy(ce * n_dp + lax.rem(dp + i, n_dp)).start()
        return 0

    lax.fori_loop(1, n_dp, send_plane, 0)
    inbuf[me] = outbuf[me]

    mate_copy.wait_recv()

    def nearest(piece):
        piece_f = piece.astype(jnp.float32)
        sq = jnp.sum(piece_f * piece_f, axis=1, keepdims=True)
        own = lax.dot_general(piece, emb_ref[...], NT, preferred_element_type=jnp.float32)
        theirs = lax.dot_general(piece, mate_rows[...], NT, preferred_element_type=jnp.float32)
        return (
            jnp.min(sq - 2.0 * own, axis=0, keepdims=True),
            jnp.min(sq - 2.0 * theirs, axis=0, keepdims=True),
        )

    def merge(a, b):
        return jnp.minimum(a[0], b[0]), jnp.minimum(a[1], b[1])

    def own_block(j, best):
        at = pl.multiple_of((j * 2 + core) * lists, lists)
        return merge(best, nearest(cent_ref[pl.ds(at, lists), :]))

    far = jnp.full((1, rows), 3e38, jnp.float32)
    best = lax.fori_loop(0, chips, own_block, (far, far))

    def plane_copy(i, block):
        other = lax.rem(chip + i, chips)
        return pltpu.make_async_remote_copy(
            src_ref=pieces.at[chip, block],
            dst_ref=pieces.at[chip, block],
            send_sem=p_send.at[other, block],
            recv_sem=p_recv.at[chip, block],
            device_id=(other * 2 + core, ce),
            device_id_type=MESH,
        )

    def arrive(ref, sem):
        return pltpu.make_async_copy(ref, ref, sem)

    order = [1, n_cent - 1] + list(range(2, n_cent - 1))
    for gap in order:
        block = lax.rem(ce + gap, n_cent)
        arrive(pieces.at[chip, block], z_recv.at[block]).wait()
        for i in range(1, chips):
            plane_copy(i, block).start()
        best = merge(best, nearest(pieces[chip, block]))
    for gap in order:
        block = lax.rem(ce + gap, n_cent)

        def other_chips(i, best):
            j = lax.rem(chip + i, chips)
            arrive(pieces.at[j, block], p_recv.at[j, block]).wait()
            return merge(best, nearest(pieces[j, block]))

        best = lax.fori_loop(1, chips, other_chips, best)

    min_out[...] = jnp.broadcast_to(best[1], min_out.shape)
    min_copy = pltpu.make_async_remote_copy(
        src_ref=min_out, dst_ref=min_in, send_sem=m_send, recv_sem=m_recv,
        device_id=(mate, ce), device_id_type=MESH,
    )
    min_copy.start()
    emb_f = emb_ref[...].astype(jnp.float32)
    row_sq = jnp.sum(emb_f * emb_f, axis=1, keepdims=True)
    row_sq = jnp.broadcast_to(row_sq, (rows, 128)).T[0:1]
    min_copy.wait()
    quant_ref[...] = (jnp.minimum(best[0], min_in[0:1]) + row_sq) * (1.0 / dim)

    def wait_rows(i, _):
        other = lax.rem(me + i, owners)
        arrive(inbuf.at[other], row_recv.at[other]).wait()
        return 0

    lax.fori_loop(1, owners, wait_rows, 0)
    own_rows = cent_ref[pl.ds(pl.multiple_of(dp * lists, lists), lists), :]
    arrived = inbuf[:, :, :dim].reshape(slots, dim)
    tags_in = inbuf[:, :, dim:].reshape(slots, TAGS).astype(jnp.float32)
    list_col = tags_in[:, 0:1].astype(jnp.int32) - 1
    bin_col = tags_in[:, 1:2].astype(jnp.int32)
    member = (lax.broadcasted_iota(jnp.int32, (slots, 128), 1) == list_col).astype(jnp.float32)
    member_t = member.T[:lists]
    member_b = member[:, :lists].astype(jnp.bfloat16)
    member_tb = member_t.astype(jnp.bfloat16)
    sums = jnp.dot(member_tb, arrived, preferred_element_type=jnp.float32)
    counts = jnp.sum(member_t, axis=1, keepdims=True)
    own_f = own_rows.astype(jnp.float32)
    new_ref[...] = own_f + (sums - counts * own_f) / jnp.maximum(counts, 1.0)
    residual = arrived.astype(jnp.float32) - jnp.dot(member_b, own_rows, preferred_element_type=jnp.float32)
    norm = jnp.sqrt(jnp.sum(residual * residual, axis=1, keepdims=True) * (1.0 / dim) + epsilon)
    in_bin = lax.broadcasted_iota(jnp.int32, (slots, NBINS), 1) == bin_col
    spread = jnp.where(in_bin, norm, 0.0)
    hist = jnp.zeros(hist_ref.shape, jnp.float32)
    for _ in range(3):
        part = spread.astype(jnp.bfloat16)
        hist = hist + jnp.dot(member_tb, part, preferred_element_type=jnp.float32)
        spread = spread - part.astype(jnp.float32)
    hist_ref[...] = hist

    mate_copy.wait_send()
    for i in range(1, n_cent):
        z_copy(i).wait_send()
    for gap in order:
        block = lax.rem(ce + gap, n_cent)
        for i in range(1, chips):
            plane_copy(i, block).wait_send()

    def sent(i, _):
        row_copy(lax.rem(me + i, owners)).wait_send()
        return 0

    lax.fori_loop(1, owners, sent, 0)


def per_device_kernel(embeddings, centroids, assign, bins):
    rows, dim = embeddings.shape
    n_dp, n_cent = lax.axis_size("dp"), lax.axis_size("cent")
    owners, chips = n_dp * n_cent, n_dp // 2
    cap = 2 * rows // owners
    lists = centroids.shape[0] // n_dp
    dma = pltpu.SemaphoreType.DMA
    vmem = pl.BlockSpec(memory_space=pltpu.VMEM)
    quant, new, hist = pl.pallas_call(
        functools.partial(kernel, n_dp, n_cent, cap),
        out_shape=(
            jax.ShapeDtypeStruct((1, rows), jnp.float32),
            jax.ShapeDtypeStruct((lists, dim), jnp.float32),
            jax.ShapeDtypeStruct((lists, NBINS), jnp.float32),
        ),
        in_specs=[vmem] * 4,
        out_specs=(vmem,) * 3,
        scratch_shapes=[
            pltpu.VMEM((owners, cap, dim + TAGS), jnp.bfloat16),
            pltpu.VMEM((owners, cap, dim + TAGS), jnp.bfloat16),
            pltpu.VMEM((rows, dim), jnp.bfloat16),
            pltpu.VMEM((chips, n_cent, lists, dim), jnp.bfloat16),
            pltpu.VMEM((8, rows), jnp.float32),
            pltpu.VMEM((8, rows), jnp.float32),
            dma((owners,)), dma((owners,)),
            dma, dma,
            dma((n_cent,)), dma((n_cent,)),
            dma((chips, n_cent)), dma((chips, n_cent)),
            dma, dma,
        ],
        compiler_params=pltpu.CompilerParams(
            collective_id=0, has_side_effects=True, vmem_limit_bytes=40 * 1024 * 1024
        ),
        cost_estimate=pl.CostEstimate(
            flops=2 * rows * 2048 * dim, bytes_accessed=4 * rows * dim * 2, transcendentals=0
        ),
    )(embeddings, centroids, assign.reshape(1, rows), bins.reshape(1, rows))
    return quant.reshape(rows), new, hist


def per_device_plain(embeddings, centroids, assign, bins):
    row_count, feature_dim = embeddings.shape
    row_f32 = embeddings.astype(jnp.float32)
    row_sq = jnp.sum(row_f32 * row_f32, axis=1)
    block_rows = lax.all_gather(centroids, "cent", axis=0, tiled=True)
    products = jnp.einsum("rd,kd->rk", embeddings, block_rows, preferred_element_type=jnp.float32)
    block_f32 = block_rows.astype(jnp.float32)
    cent_sq = jnp.sum(block_f32 * block_f32, axis=1)
    nearest_sq = jnp.min(cent_sq[None, :] - 2.0 * products, axis=1)
    quant_error = (nearest_sq + row_sq) / feature_dim
    dp_count = lax.axis_size("dp")
    cent_count = lax.axis_size("cent")
    owner_count = dp_count * cent_count
    slot_cap = 2 * row_count // owner_count
    owner_id = assign // LISTS_DEV
    local_list = assign % LISTS_DEV
    dest_slot = owner_id % dp_count * cent_count + owner_id // dp_count
    owner_hits = (dest_slot[:, None] == jnp.arange(owner_count, dtype=jnp.int32)[None, :]).astype(jnp.float32)
    row_ids = jnp.arange(row_count, dtype=jnp.int32)
    before = (row_ids[None, :] < row_ids[:, None]).astype(jnp.float32)
    earlier = jnp.dot(before, owner_hits)
    slot_id = jnp.sum(earlier * owner_hits, axis=1).astype(jnp.int32)
    position = dest_slot * slot_cap + slot_id
    outgoing = jnp.zeros((owner_count * slot_cap, feature_dim), jnp.bfloat16).at[position].set(embeddings)
    outgoing = outgoing.reshape(dp_count, cent_count, slot_cap, feature_dim)
    tag_values = jnp.stack([local_list, bins], axis=1).astype(jnp.float32)
    labels = jnp.full((owner_count * slot_cap, 2), -1.0, jnp.float32).at[position].set(tag_values)
    labels = labels.astype(jnp.bfloat16).reshape(dp_count, cent_count, slot_cap, 2)

    def exchange(x):
        x = lax.all_to_all(x, "dp", split_axis=0, concat_axis=0, tiled=True)
        return lax.all_to_all(x, "cent", split_axis=1, concat_axis=1, tiled=True)

    arrived = exchange(outgoing).reshape(-1, feature_dim).astype(jnp.float32)
    arrived_tags = exchange(labels).reshape(-1, 2).astype(jnp.int32)
    list_ids, bin_ids = arrived_tags[:, 0], arrived_tags[:, 1]
    member = (list_ids[:, None] == jnp.arange(LISTS_DEV, dtype=jnp.int32)[None, :]).astype(jnp.float32)
    own_rows = lax.dynamic_slice_in_dim(
        centroids, lax.axis_index("dp") * LISTS_DEV, LISTS_DEV, 0
    ).astype(jnp.float32)
    highest = lax.Precision.HIGHEST
    residual = arrived - jnp.dot(member, own_rows, precision=highest)
    residual_sums = jnp.dot(member.T, residual, precision=highest)
    counts = jnp.sum(member, axis=0)
    updated = own_rows + residual_sums / jnp.maximum(counts, 1.0)[:, None]
    residual_norm = jnp.sqrt(jnp.mean(residual * residual, axis=1) + epsilon)
    bin_hits = (bin_ids[:, None] == jnp.arange(NBINS, dtype=jnp.int32)[None, :]).astype(jnp.float32)
    histogram = jnp.dot(member.T, bin_hits * residual_norm[:, None], precision=highest)
    return (quant_error, updated, histogram)


def per_device(embeddings, centroids, assign, bins):
    owner_count = lax.axis_size("dp") * lax.axis_size("cent")
    if (2 * embeddings.shape[0] // owner_count) % 16 == 0:
        return per_device_kernel(embeddings, centroids, assign, bins)
    return per_device_plain(embeddings, centroids, assign, bins)


def solution(mesh):
    in_specs = (P(("dp", "cent"), None), P("cent", None), P(("dp", "cent")), P(("dp", "cent")))
    out_specs = (P(("dp", "cent")), P(("cent", "dp"), None), P(("cent", "dp"), None))
    return jax.shard_map(
        per_device, mesh=mesh, in_specs=in_specs, out_specs=out_specs, check_vma=False
    )
```

time: 107 us -> 51.8 us (0.48)
  the two profiles are of different devices: /device:TPU:0 before, /device:TPU:11 now
where the time goes in v1:
time: 51.8 us; the launch traced here: 51.6 us
  Pallas kernels  46.2 us (89%)
  local copies, waits for them, and re-layouts  4.68 us (9%)
  between operations  0.66 us (1%)
    pallas_call x1, Pallas kernels, per_device_kernel(): pl.pallas_call(functools.partial(kernel, n_dp, n_cent, cap), out_shape=(j...  46.2 us
    unnamed x11, local copies, waits for them, and re-layouts  4.68 us

profile of v1, /device:TPU:11, one launch (start us, length us, event | category | flops | bytes accessed | tf_op | source)
XLA Modules:
  0.0 51.6 jit_solution(16679929587027495466)
XLA Ops:
  0.6 0.0 copy-start.3
  0.6 0.0 copy-start.2
  0.7 0.7 %copy-done.3 = s32[256]{0:T(256)S(1)} copy-done((s32[256]{0:T(256)S(1)}, s32[256]{0:T(256)}, u32[]{:S(2)}) %copy-start.3) | copy-done | bytes 1048
  1.3 0.0 copy-done.2
  1.3 0.0 copy-start
  1.3 1.1 %copy-done = bf16[512,768]{1,0:T(8,128)(2,1)S(1)} copy-done((bf16[512,768]{1,0:T(8,128)(2,1)S(1)}, bf16[512,768]{1,0:T(8,128)(2,1)}, u32[]{:S(2)}) %copy-start) | copy-done | bytes 786456
  2.5 0.0 copy-start.1
  2.5 1.0 %copy-done.1 = bf16[256,768]{1,0:T(8,128)(2,1)S(1)} copy-done((bf16[256,768]{1,0:T(8,128)(2,1)S(1)}, bf16[256,768]{1,0:T(8,128)(2,1)}, u32[]{:S(2)}) %copy-start.1) | copy-done | bytes 393240
  3.5 46.2 %shard_map.67 = (f32[1,256]{1,0:T(1,128)S(1)}, f32[64,768]{1,0:T(8,128)S(1)}, f32[64,256]{1,0:T(8,128)S(1)}) custom-call(bf16[256,768]{1,0:T(8,128)(2,1)S(1)} %copy-done.1, bf16[512,768]{1,0:T(8,128)(2,1)S(1)} %copy-done, s32[1,256]{1,0:T(1,128)S(1)} %bitcast.4, s32[1,256]{1,0:T(1,128)S(1)} %bitcast.5), custom_call_target="tpu_custom_call" | custom-call | flops 805306368 | bytes 1572864 | tf_op jit(solution)/shard_map/pallas_call | solution.py:239
  49.7 0.6 %copy.10 = f32[256]{0:T(256)} copy(f32[256]{0:T(256)S(1)} %bitcast.3) | data formatting | bytes 2048
  50.3 0.7 %copy.11 = f32[64,768]{1,0:T(8,128)} copy(f32[64,768]{1,0:T(8,128)S(1)} %get-tuple-element.13) | data formatting | bytes 393216
  51.0 0.6 %copy.12 = f32[64,256]{1,0:T(8,128)} copy(f32[64,256]{1,0:T(8,128)S(1)} %get-tuple-element.14) | data formatting | bytes 131072
Async XLA Ops:
  0.6 0.7 %copy-start.3 = (s32[256]{0:T(256)S(1)}, s32[256]{0:T(256)}, u32[]{:S(2)}) copy-start(s32[256]{0:T(256)} %param.7) | copy-start | bytes 3076
  0.6 0.7 %copy-start.2 = (s32[256]{0:T(256)S(1)}, s32[256]{0:T(256)}, u32[]{:S(2)}) copy-start(s32[256]{0:T(256)} %param.6) | copy-start | bytes 3076
  1.3 1.1 %copy-start = (bf16[512,768]{1,0:T(8,128)(2,1)S(1)}, bf16[512,768]{1,0:T(8,128)(2,1)}, u32[]{:S(2)}) copy-start(bf16[512,768]{1,0:T(8,128)(2,1)} %cent_ref.1) | copy-start | bytes 2359300
  2.5 1.0 %copy-start.1 = (bf16[256,768]{1,0:T(8,128)(2,1)S(1)}, bf16[256,768]{1,0:T(8,128)(2,1)}, u32[]{:S(2)}) copy-start(bf16[256,768]{1,0:T(8,128)(2,1)} %emb_ref.1) | copy-start | bytes 1179652

commit v2 on v1

--- a/solution.py
+++ b/solution.py
@@ -9,7 +9,6 @@
 
 LISTS_DEV = 64
 NBINS = 256
-TAGS = 128
 
 epsilon = 1e-06
 MESH = pl.DeviceIdType.MESH
@@ -18,21 +17,37 @@
 
 def kernel(
     n_dp, n_cent, cap,
-    emb_ref, cent_ref, assign_ref, bins_ref,
+    emb_hbm, cent_hbm, assign_hbm, bins_hbm,
     quant_ref, new_ref, hist_ref,
-    outbuf, inbuf, mate_rows, pieces, min_out, min_in,
+    assign_ref, bins_ref, emb_ref, outbuf, inbuf, mate_rows, pieces, min_out, min_in, code_out, code_z, codes,
+    in_sem, own_sem,
     row_send, row_recv, mate_send, mate_recv, z_send, z_recv, p_send, p_recv, m_send, m_recv,
+    cz_send, cz_recv, cp_send, cp_recv,
 ):
     rows, dim = emb_ref.shape
-    lists = cent_ref.shape[0] // n_dp
-    chips = n_dp // 2
+    chips, lists = pieces.shape[1], pieces.shape[2]
     owners = n_dp * n_cent
     slots = owners * cap
+    width = n_dp * cap
     dp, ce = lax.axis_index("dp"), lax.axis_index("cent")
     chip, core = dp // 2, dp % 2
     mate = chip * 2 + (1 - core)
     me = ce * n_dp + dp
 
+    loads = [
+        pltpu.make_async_copy(a, b, in_sem.at[n])
+        for n, (a, b) in enumerate(((assign_hbm, assign_ref), (bins_hbm, bins_ref), (emb_hbm, emb_ref)))
+    ]
+    for load in loads:
+        load.start()
+
+    def share(j):
+        at = pl.multiple_of((j * 2 + core) * lists, lists)
+        return pltpu.make_async_copy(cent_hbm.at[pl.ds(at, lists)], pieces.at[ce, j], own_sem.at[j])
+
+    for j in range(chips):
+        share(j).start()
+
     barrier = pltpu.get_barrier_semaphore()
 
     def greet(i, _):
@@ -41,6 +56,10 @@
         return 0
 
     lax.fori_loop(1, owners, greet, 0)
+    for load in loads:
+        load.wait()
+    for j in range(chips):
+        share(j).wait()
 
     shift = lists.bit_length() - 1
     assign = assign_ref[...]
@@ -57,51 +76,75 @@
     place = jnp.sum(earlier * hits_f, axis=0, keepdims=True)
     position = owner * cap + place.astype(jnp.int32)
     pick = (lax.broadcasted_iota(jnp.int32, (slots, rows), 0) == position).astype(jnp.float32).astype(jnp.bfloat16)
-    tag_row = lax.broadcasted_iota(jnp.int32, (TAGS, rows), 0)
+    tag_row = lax.broadcasted_iota(jnp.int32, (16, rows), 0)
     tags = jnp.where(
         tag_row == 0,
-        jnp.broadcast_to(local + 1, (TAGS, rows)),
-        jnp.where(tag_row == 1, jnp.broadcast_to(bins_ref[...], (TAGS, rows)), 0),
+        jnp.broadcast_to(local + 1, (16, rows)),
+        jnp.where(tag_row == 1, jnp.broadcast_to(bins_ref[...], (16, rows)), 0),
     ).astype(jnp.float32).astype(jnp.bfloat16)
-    outbuf[:, :, :dim] = (
+    outbuf[...] = (
         jnp.dot(pick, emb_ref[...], preferred_element_type=jnp.float32)
         .astype(jnp.bfloat16).reshape(owners, cap, dim)
     )
-    outbuf[:, :, dim:] = (
-        lax.dot_general(pick, tags, NT, preferred_element_type=jnp.float32)
-        .astype(jnp.bfloat16).reshape(owners, cap, TAGS)
-    )
+    slot_tags = lax.dot_general(tags, pick, NT, preferred_element_type=jnp.float32).astype(jnp.int32)
+    code = slot_tags[0:1] * NBINS + slot_tags[1:2]
+    for c in range(n_cent):
+        code_out[c] = code[:, c * width:(c + 1) * width]
 
     pl.semaphore_wait(barrier, owners - 1)
 
     def z_copy(i):
         other = lax.rem(ce + i, n_cent)
         return pltpu.make_async_remote_copy(
-            src_ref=cent_ref.at[pl.ds(pl.multiple_of(dp * lists, lists), lists)],
-            dst_ref=pieces.at[chip, ce],
-            send_sem=z_send.at[other],
-            recv_sem=z_recv.at[ce],
-            device_id=(dp, other),
-            device_id_type=MESH,
-        )
-
-    for i in range(1, n_cent):
+            src_ref=pieces.at[ce, chip], dst_ref=pieces.at[ce, chip],
+            send_sem=z_send.at[other], recv_sem=z_recv.at[ce],
+            device_id=(dp, other), device_id_type=MESH,
+        )
+
+    def code_copy(i):
+        other = lax.rem(ce + i, n_cent)
+        return pltpu.make_async_remote_copy(
+            src_ref=code_out.at[other], dst_ref=code_z.at[ce],
+            send_sem=cz_send.at[other], recv_sem=cz_recv.at[ce],
+            device_id=(dp, other), device_id_type=MESH,
+        )
+
+    def row_copy(other):
+        return pltpu.make_async_remote_copy(
+            src_ref=outbuf.at[other], dst_ref=inbuf.at[me],
+            send_sem=row_send.at[other], recv_sem=row_recv.at[me],
+            device_id=(other % n_dp, other // n_dp), device_id_type=MESH,
+        )
+
+    order = list(range(1, n_cent))
+    for i in order:
         z_copy(i).start()
+    for i in order:
+        code_copy(i).start()
     mate_copy = pltpu.make_async_remote_copy(
         src_ref=emb_ref, dst_ref=mate_rows, send_sem=mate_send, recv_sem=mate_recv,
         device_id=(mate, ce), device_id_type=MESH,
     )
     mate_copy.start()
 
-    def row_copy(other):
-        return pltpu.make_async_remote_copy(
-            src_ref=outbuf.at[other],
-            dst_ref=inbuf.at[me],
-            send_sem=row_send.at[other],
-            recv_sem=row_recv.at[me],
-            device_id=(other % n_dp, other // n_dp),
-            device_id_type=MESH,
-        )
+    def send_plane(i, _):
+        row_copy(ce * n_dp + lax.rem(dp + i, n_dp)).start()
+        return 0
+
+    lax.fori_loop(1, n_dp, send_plane, 0)
+    inbuf[me] = outbuf[me]
+    code_z[ce] = code_out[ce]
+
+    def plane_copy(i, block):
+        other = lax.rem(chip + i, chips)
+        return pltpu.make_async_remote_copy(
+            src_ref=pieces.at[block, chip], dst_ref=pieces.at[block, chip],
+            send_sem=p_send.at[block, other], recv_sem=p_recv.at[block, chip],
+            device_id=(other * 2 + core, ce), device_id_type=MESH,
+        )
+
+    def arrive(ref, sem):
+        return pltpu.make_async_copy(ref, ref, sem)
 
     def send_rows(i, _):
         gap = i // n_dp + 1
@@ -109,18 +152,33 @@
         row_copy(other).start()
         return 0
 
-    lax.fori_loop(0, owners - n_dp, send_rows, 0)
-
-    def send_plane(i, _):
-        row_copy(ce * n_dp + lax.rem(dp + i, n_dp)).start()
-        return 0
-
-    lax.fori_loop(1, n_dp, send_plane, 0)
-    inbuf[me] = outbuf[me]
+    for gap in order:
+        block = lax.rem(ce + gap, n_cent)
+        arrive(pieces.at[block, chip], z_recv.at[block]).wait()
+        for i in range(1, chips):
+            plane_copy(i, block).start()
+        lax.fori_loop((gap - 1) * n_dp, gap * n_dp, send_rows, 0)
+
+
+    def spread_copy(i):
+        other = lax.rem(dp + i, n_dp)
+        return pltpu.make_async_remote_copy(
+            src_ref=code_z, dst_ref=codes.at[dp],
+            send_sem=cp_send.at[other], recv_sem=cp_recv.at[dp],
+            device_id=(other, ce), device_id_type=MESH,
+        )
+
+    for gap in order:
+        block = lax.rem(ce + gap, n_cent)
+        arrive(code_z.at[block], cz_recv.at[block]).wait()
+    for i in range(1, n_dp):
+        spread_copy(i).start()
+    codes[dp] = code_z[...]
 
     mate_copy.wait_recv()
 
-    def nearest(piece):
+    def nearest(block):
+        piece = pieces[block].reshape(chips * lists, dim)
         piece_f = piece.astype(jnp.float32)
         sq = jnp.sum(piece_f * piece_f, axis=1, keepdims=True)
         own = lax.dot_general(piece, emb_ref[...], NT, preferred_element_type=jnp.float32)
@@ -130,46 +188,20 @@
             jnp.min(sq - 2.0 * theirs, axis=0, keepdims=True),
         )
 
-    def merge(a, b):
-        return jnp.minimum(a[0], b[0]), jnp.minimum(a[1], b[1])
-
-    def own_block(j, best):
-        at = pl.multiple_of((j * 2 + core) * lists, lists)
-        return merge(best, nearest(cent_ref[pl.ds(at, lists), :]))
-
-    far = jnp.full((1, rows), 3e38, jnp.float32)
-    best = lax.fori_loop(0, chips, own_block, (far, far))
-
-    def plane_copy(i, block):
-        other = lax.rem(chip + i, chips)
-        return pltpu.make_async_remote_copy(
-            src_ref=pieces.at[chip, block],
-            dst_ref=pieces.at[chip, block],
-            send_sem=p_send.at[other, block],
-            recv_sem=p_recv.at[chip, block],
-            device_id=(other * 2 + core, ce),
-            device_id_type=MESH,
-        )
-
-    def arrive(ref, sem):
-        return pltpu.make_async_copy(ref, ref, sem)
-
-    order = [1, n_cent - 1] + list(range(2, n_cent - 1))
-    for gap in order:
+    best = nearest(ce)
+    emb_f = emb_ref[...].astype(jnp.float32)
+    row_sq = jnp.sum(emb_f * emb_f, axis=1, keepdims=True)
+    row_sq = jnp.broadcast_to(row_sq, (rows, 128)).T[0:1]
+
+    def one_block(gap, best):
         block = lax.rem(ce + gap, n_cent)
-        arrive(pieces.at[chip, block], z_recv.at[block]).wait()
         for i in range(1, chips):
-            plane_copy(i, block).start()
-        best = merge(best, nearest(pieces[chip, block]))
-    for gap in order:
-        block = lax.rem(ce + gap, n_cent)
-
-        def other_chips(i, best):
             j = lax.rem(chip + i, chips)
-            arrive(pieces.at[j, block], p_recv.at[j, block]).wait()
-            return merge(best, nearest(pieces[j, block]))
-
-        best = lax.fori_loop(1, chips, other_chips, best)
+            arrive(pieces.at[block, j], p_recv.at[block, j]).wait()
+        found = nearest(block)
+        return jnp.minimum(best[0], found[0]), jnp.minimum(best[1], found[1])
+
+    best = lax.fori_loop(1, n_cent, one_block, best)
 
     min_out[...] = jnp.broadcast_to(best[1], min_out.shape)
     min_copy = pltpu.make_async_remote_copy(
@@ -177,34 +209,53 @@
         device_id=(mate, ce), device_id_type=MESH,
     )
     min_copy.start()
-    emb_f = emb_ref[...].astype(jnp.float32)
-    row_sq = jnp.sum(emb_f * emb_f, axis=1, keepdims=True)
-    row_sq = jnp.broadcast_to(row_sq, (rows, 128)).T[0:1]
-    min_copy.wait()
-    quant_ref[...] = (jnp.minimum(best[0], min_in[0:1]) + row_sq) * (1.0 / dim)
-
-    def wait_rows(i, _):
-        other = lax.rem(me + i, owners)
-        arrive(inbuf.at[other], row_recv.at[other]).wait()
-        return 0
-
-    lax.fori_loop(1, owners, wait_rows, 0)
-    own_rows = cent_ref[pl.ds(pl.multiple_of(dp * lists, lists), lists), :]
-    arrived = inbuf[:, :, :dim].reshape(slots, dim)
-    tags_in = inbuf[:, :, dim:].reshape(slots, TAGS).astype(jnp.float32)
-    list_col = tags_in[:, 0:1].astype(jnp.int32) - 1
-    bin_col = tags_in[:, 1:2].astype(jnp.int32)
+
+    for i in range(1, n_dp):
+        other = lax.rem(dp + i, n_dp)
+        arrive(codes.at[other], cp_recv.at[other]).wait()
+    every = jnp.concatenate([codes[d, c] for c in range(n_cent) for d in range(n_dp)], axis=0)
+    list_tag = lax.shift_right_logical(every, 8)
+    bin_tag = every - lax.shift_left(list_tag, 8)
+    slot = lax.broadcasted_iota(jnp.int32, (slots, owners), 0)
+    source = lax.broadcasted_iota(jnp.int32, (slots, owners), 1)
+    low = slot - source * cap
+    of_source = ((low >= 0) & (low < cap)).astype(jnp.float32).astype(jnp.bfloat16)
+    lane = lax.broadcasted_iota(jnp.int32, (slots, width), 1)
+    row_id = lax.broadcasted_iota(jnp.int32, (slots, width), 0)
+    mine = lane == dp * cap + lax.rem(row_id, cap)
+
+    def column(tag):
+        spread = jnp.dot(
+            of_source, tag.astype(jnp.float32).astype(jnp.bfloat16), preferred_element_type=jnp.float32
+        )
+        return jnp.sum(jnp.where(mine, spread, 0.0), axis=1, keepdims=True).astype(jnp.int32)
+
+    list_col = column(list_tag) - 1
+    bin_col = column(bin_tag)
     member = (lax.broadcasted_iota(jnp.int32, (slots, 128), 1) == list_col).astype(jnp.float32)
     member_t = member.T[:lists]
     member_b = member[:, :lists].astype(jnp.bfloat16)
     member_tb = member_t.astype(jnp.bfloat16)
+    counts = jnp.sum(member_t, axis=1, keepdims=True)
+    in_bin = lax.broadcasted_iota(jnp.int32, (slots, NBINS), 1) == bin_col
+    own_rows = pieces[ce, chip]
+    own_f = own_rows.astype(jnp.float32)
+    own_spread = jnp.dot(member_b, own_rows, preferred_element_type=jnp.float32)
+
+    min_copy.wait()
+    quant_ref[...] = (jnp.minimum(best[0], min_in[0:1]) + row_sq) * (1.0 / dim)
+
+    def wait_rows(i, _):
+        other = lax.rem(me + i, owners)
+        arrive(inbuf.at[other], row_recv.at[other]).wait()
+        return 0
+
+    lax.fori_loop(1, owners, wait_rows, 0)
+    arrived = inbuf[...].reshape(slots, dim)
     sums = jnp.dot(member_tb, arrived, preferred_element_type=jnp.float32)
-    counts = jnp.sum(member_t, axis=1, keepdims=True)
-    own_f = own_rows.astype(jnp.float32)
     new_ref[...] = own_f + (sums - counts * own_f) / jnp.maximum(counts, 1.0)
-    residual = arrived.astype(jnp.float32) - jnp.dot(member_b, own_rows, preferred_element_type=jnp.float32)
+    residual = arrived.astype(jnp.float32) - own_spread
     norm = jnp.sqrt(jnp.sum(residual * residual, axis=1, keepdims=True) * (1.0 / dim) + epsilon)
-    in_bin = lax.broadcasted_iota(jnp.int32, (slots, NBINS), 1) == bin_col
     spread = jnp.where(in_bin, norm, 0.0)
     hist = jnp.zeros(hist_ref.shape, jnp.float32)
     for _ in range(3):
@@ -214,12 +265,13 @@
     hist_ref[...] = hist
 
     mate_copy.wait_send()
-    for i in range(1, n_cent):
+    for i in order:
         z_copy(i).wait_send()
-    for gap in order:
-        block = lax.rem(ce + gap, n_cent)
-        for i in range(1, chips):
-            plane_copy(i, block).wait_send()
+        code_copy(i).wait_send()
+        for k in range(1, chips):
+            plane_copy(k, lax.rem(ce + i, n_cent)).wait_send()
+    for i in range(1, n_dp):
+        spread_copy(i).wait_send()
 
     def sent(i, _):
         row_copy(lax.rem(me + i, owners)).wait_send()
@@ -243,23 +295,32 @@
             jax.ShapeDtypeStruct((lists, dim), jnp.float32),
             jax.ShapeDtypeStruct((lists, NBINS), jnp.float32),
         ),
-        in_specs=[vmem] * 4,
+        in_specs=[pl.BlockSpec(memory_space=pltpu.HBM)] * 4,
         out_specs=(vmem,) * 3,
         scratch_shapes=[
-            pltpu.VMEM((owners, cap, dim + TAGS), jnp.bfloat16),
-            pltpu.VMEM((owners, cap, dim + TAGS), jnp.bfloat16),
+            pltpu.VMEM((1, rows), jnp.int32),
+            pltpu.VMEM((1, rows), jnp.int32),
             pltpu.VMEM((rows, dim), jnp.bfloat16),
-            pltpu.VMEM((chips, n_cent, lists, dim), jnp.bfloat16),
+            pltpu.VMEM((owners, cap, dim), jnp.bfloat16),
+            pltpu.VMEM((owners, cap, dim), jnp.bfloat16),
+            pltpu.VMEM((rows, dim), jnp.bfloat16),
+            pltpu.VMEM((n_cent, chips, lists, dim), jnp.bfloat16),
             pltpu.VMEM((8, rows), jnp.float32),
             pltpu.VMEM((8, rows), jnp.float32),
+            pltpu.VMEM((n_cent, 1, n_dp * cap), jnp.int32),
+            pltpu.VMEM((n_cent, 1, n_dp * cap), jnp.int32),
+            pltpu.VMEM((n_dp, n_cent, 1, n_dp * cap), jnp.int32),
+            dma((3,)), dma((chips,)),
             dma((owners,)), dma((owners,)),
             dma, dma,
             dma((n_cent,)), dma((n_cent,)),
-            dma((chips, n_cent)), dma((chips, n_cent)),
+            dma((n_cent, chips)), dma((n_cent, chips)),
             dma, dma,
+            dma((n_cent,)), dma((n_cent,)),
+            dma((n_dp,)), dma((n_dp,)),
         ],
         compiler_params=pltpu.CompilerParams(
-            collective_id=0, has_side_effects=True, vmem_limit_bytes=40 * 1024 * 1024
+            collective_id=0, has_side_effects=True, vmem_limit_bytes=60 * 1024 * 1024
         ),
         cost_estimate=pl.CostEstimate(
             flops=2 * rows * 2048 * dim, bytes_accessed=4 * rows * dim * 2, transcendentals=0
@@ -320,8 +381,9 @@
 
 
 def per_device(embeddings, centroids, assign, bins):
-    owner_count = lax.axis_size("dp") * lax.axis_size("cent")
-    if (2 * embeddings.shape[0] // owner_count) % 16 == 0:
+    n_dp = lax.axis_size("dp")
+    cap = 2 * embeddings.shape[0] // (n_dp * lax.axis_size("cent"))
+    if cap % 16 == 0 and n_dp * cap % 128 == 0:
         return per_device_kernel(embeddings, centroids, assign, bins)
     return per_device_plain(embeddings, centroids, assign, bins)
 

time: 51.8 us -> 43.5 us (0.84)
  Pallas kernels: 46.2 us -> 39.2 us
  local copies, waits for them, and re-layouts: 4.68 us -> 3.51 us
    pallas_call x1, Pallas kernels: 46.2 us -> 39.2 us  [per_device_kernel(): pl.pallas_call(functools.partial(kernel, n_dp, n_cent, cap), out_shape=(j...]
    unnamed x11 -> x7, local copies, waits for them, and re-layouts: 4.68 us -> 3.51 us
where the time goes in v2:
time: 43.5 us; the launch traced here: 43.3 us
  Pallas kernels  39.2 us (90%)
  local copies, waits for them, and re-layouts  3.51 us (8%)
  between operations  0.65 us (1%)
    pallas_call x1, Pallas kernels, per_device_kernel(): pl.pallas_call(functools.partial(kernel, n_dp, n_cent, cap), out_shape=(j...  39.2 us
    unnamed x7, local copies, waits for them, and re-layouts  3.51 us

profile of v2, /device:TPU:11, one launch (start us, length us, event | category | flops | bytes accessed | tf_op | source)
XLA Modules:
  0.0 43.3 jit_solution(14713374754636052324)
XLA Ops:
  0.6 39.2 %shard_map.67 = (f32[1,256]{1,0:T(1,128)}, f32[64,768]{1,0:T(8,128)}, f32[64,256]{1,0:T(8,128)}) custom-call(bf16[256,768]{1,0:T(8,128)(2,1)} %emb_hbm.1, bf16[512,768]{1,0:T(8,128)(2,1)} %cent_hbm.1, s32[1,256]{1,0:T(1,128)} %bitcast.4, s32[1,256]{1,0:T(1,128)} %bitcast.5), custom_call_target="tpu_custom_call" | custom-call | flops 805306368 | bytes 1572864 | tf_op jit(solution)/shard_map/pallas_call | solution.py:291
  39.8 0.0 copy-start.1
  39.8 0.7 %copy-done.1 = f32[1,256]{1,0:T(1,128)S(1)} copy-done((f32[1,256]{1,0:T(1,128)S(1)}, f32[1,256]{1,0:T(1,128)}, u32[]{:S(2)}) %copy-start.1) | copy-done | bytes 1048
  40.5 0.6 %copy.10 = f32[256]{0:T(256)} copy(f32[256]{0:T(256)S(1)} %bitcast.3) | data formatting | bytes 2048
  41.0 0.0 copy-start
  41.0 1.6 %copy.11 = f32[64,768]{1,0:T(8,128)} copy(f32[64,768]{1,0:T(8,128)} %get-tuple-element.13) | data formatting | bytes 393216
  42.7 0.0 copy-done
  42.7 0.6 %copy.12 = f32[64,256]{1,0:T(8,128)} copy(f32[64,256]{1,0:T(8,128)S(1)} %copy-done) | data formatting | bytes 131072
Async XLA Ops:
  39.8 0.7 %copy-start.1 = (f32[1,256]{1,0:T(1,128)S(1)}, f32[1,256]{1,0:T(1,128)}, u32[]{:S(2)}) copy-start(f32[1,256]{1,0:T(1,128)} %get-tuple-element.6) | copy-start | bytes 3076
  41.0 1.7 %copy-start = (f32[64,256]{1,0:T(8,128)S(1)}, f32[64,256]{1,0:T(8,128)}, u32[]{:S(2)}) copy-start(f32[64,256]{1,0:T(8,128)} %get-tuple-element.14) | copy-start | bytes 196612

commit v3 on v2

--- a/solution.py
+++ b/solution.py
@@ -19,19 +19,22 @@
     n_dp, n_cent, cap,
     emb_hbm, cent_hbm, assign_hbm, bins_hbm,
     quant_ref, new_ref, hist_ref,
-    assign_ref, bins_ref, emb_ref, outbuf, inbuf, mate_rows, pieces, min_out, min_in, code_out, code_z, codes,
+    assign_ref, bins_ref, group, outbuf, inbuf, pieces, min_out, min_in, code_out, code_z, codes,
     in_sem, own_sem,
-    row_send, row_recv, mate_send, mate_recv, z_send, z_recv, p_send, p_recv, m_send, m_recv,
+    row_send, row_recv, g_send, g_recv, up_send, down_send, z_recv, y_send, y_recv, m_send, m_recv,
     cz_send, cz_recv, cp_send, cp_recv,
 ):
-    rows, dim = emb_ref.shape
-    chips, lists = pieces.shape[1], pieces.shape[2]
+    rows, dim = group.shape[1:]
+    span, lists = pieces.shape[1], pieces.shape[2]
     owners = n_dp * n_cent
     slots = owners * cap
     width = n_dp * cap
     dp, ce = lax.axis_index("dp"), lax.axis_index("cent")
-    chip, core = dp // 2, dp % 2
-    mate = chip * 2 + (1 - core)
+    y, x, core = dp // 4, (dp // 2) % 2, dp % 2
+    mate = y * 4 + x * 2 + (1 - core)
+    beside = y * 4 + (1 - x) * 2 + core
+    across = y * 4 + (1 - x) * 2 + (1 - core)
+    emb_ref = group.at[3]
     me = ce * n_dp + dp
 
     loads = [
@@ -42,10 +45,10 @@
         load.start()
 
     def share(j):
-        at = pl.multiple_of((j * 2 + core) * lists, lists)
+        at = pl.multiple_of(((j * 2 + x) * 2 + core) * lists, lists)
         return pltpu.make_async_copy(cent_hbm.at[pl.ds(at, lists)], pieces.at[ce, j], own_sem.at[j])
 
-    for j in range(chips):
+    for j in range(span):
         share(j).start()
 
     barrier = pltpu.get_barrier_semaphore()
@@ -58,7 +61,7 @@
     lax.fori_loop(1, owners, greet, 0)
     for load in loads:
         load.wait()
-    for j in range(chips):
+    for j in range(span):
         share(j).wait()
 
     shift = lists.bit_length() - 1
@@ -93,12 +96,11 @@
 
     pl.semaphore_wait(barrier, owners - 1)
 
-    def z_copy(i):
-        other = lax.rem(ce + i, n_cent)
-        return pltpu.make_async_remote_copy(
-            src_ref=pieces.at[ce, chip], dst_ref=pieces.at[ce, chip],
-            send_sem=z_send.at[other], recv_sem=z_recv.at[ce],
-            device_id=(dp, other), device_id_type=MESH,
+    def z_copy(block, step, sems):
+        return pltpu.make_async_remote_copy(
+            src_ref=pieces.at[block, y], dst_ref=pieces.at[block, y],
+            send_sem=sems.at[block], recv_sem=z_recv.at[block],
+            device_id=(dp, ce + step), device_id_type=MESH,
         )
 
     def code_copy(i):
@@ -117,15 +119,27 @@
         )
 
     order = list(range(1, n_cent))
-    for i in order:
-        z_copy(i).start()
+
+    @pl.when(ce + 1 < n_cent)
+    def _():
+        z_copy(ce, 1, up_send).start()
+
+    @pl.when(ce > 0)
+    def _():
+        z_copy(ce, -1, down_send).start()
+
     for i in order:
         code_copy(i).start()
-    mate_copy = pltpu.make_async_remote_copy(
-        src_ref=emb_ref, dst_ref=mate_rows, send_sem=mate_send, recv_sem=mate_recv,
-        device_id=(mate, ce), device_id_type=MESH,
-    )
-    mate_copy.start()
+
+    def group_copy(source, slot, other):
+        return pltpu.make_async_remote_copy(
+            src_ref=group.at[source], dst_ref=group.at[slot],
+            send_sem=g_send.at[slot], recv_sem=g_recv.at[slot],
+            device_id=(other, ce), device_id_type=MESH,
+        )
+
+    group_copy(3, 1, beside).start()
+    group_copy(3, 0, mate).start()
 
     def send_plane(i, _):
         row_copy(ce * n_dp + lax.rem(dp + i, n_dp)).start()
@@ -135,12 +149,12 @@
     inbuf[me] = outbuf[me]
     code_z[ce] = code_out[ce]
 
-    def plane_copy(i, block):
-        other = lax.rem(chip + i, chips)
-        return pltpu.make_async_remote_copy(
-            src_ref=pieces.at[block, chip], dst_ref=pieces.at[block, chip],
-            send_sem=p_send.at[block, other], recv_sem=p_recv.at[block, chip],
-            device_id=(other * 2 + core, ce), device_id_type=MESH,
+    def y_copy(i, block):
+        other = lax.rem(y + i, span)
+        return pltpu.make_async_remote_copy(
+            src_ref=pieces.at[block, y], dst_ref=pieces.at[block, y],
+            send_sem=y_send.at[block, other], recv_sem=y_recv.at[block, y],
+            device_id=(other * 4 + x * 2 + core, ce), device_id_type=MESH,
         )
 
     def arrive(ref, sem):
@@ -153,12 +167,33 @@
         return 0
 
     for gap in order:
-        block = lax.rem(ce + gap, n_cent)
-        arrive(pieces.at[block, chip], z_recv.at[block]).wait()
-        for i in range(1, chips):
-            plane_copy(i, block).start()
-        lax.fori_loop((gap - 1) * n_dp, gap * n_dp, send_rows, 0)
-
+
+        @pl.when(ce >= gap)
+        def _():
+            block = ce - gap
+            arrive(pieces.at[block, y], z_recv.at[block]).wait()
+
+            @pl.when(ce + 1 < n_cent)
+            def _():
+                z_copy(block, 1, up_send).start()
+
+            for i in range(1, span):
+                y_copy(i, block).start()
+
+        @pl.when(ce + gap < n_cent)
+        def _():
+            block = ce + gap
+            arrive(pieces.at[block, y], z_recv.at[block]).wait()
+
+            @pl.when(ce > 0)
+            def _():
+                z_copy(block, -1, down_send).start()
+
+            for i in range(1, span):
+                y_copy(i, block).start()
+
+
+    lax.fori_loop(0, owners - n_dp, send_rows, 0)
 
     def spread_copy(i):
         other = lax.rem(dp + i, n_dp)
@@ -175,18 +210,17 @@
         spread_copy(i).start()
     codes[dp] = code_z[...]
 
-    mate_copy.wait_recv()
+    arrive(group.at[1], g_recv.at[1]).wait()
+    group_copy(1, 2, mate).start()
+    arrive(group.at[0], g_recv.at[0]).wait()
+    arrive(group.at[2], g_recv.at[2]).wait()
 
     def nearest(block):
-        piece = pieces[block].reshape(chips * lists, dim)
+        piece = pieces[block].reshape(span * lists, dim)
         piece_f = piece.astype(jnp.float32)
         sq = jnp.sum(piece_f * piece_f, axis=1, keepdims=True)
-        own = lax.dot_general(piece, emb_ref[...], NT, preferred_element_type=jnp.float32)
-        theirs = lax.dot_general(piece, mate_rows[...], NT, preferred_element_type=jnp.float32)
-        return (
-            jnp.min(sq - 2.0 * own, axis=0, keepdims=True),
-            jnp.min(sq - 2.0 * theirs, axis=0, keepdims=True),
-        )
+        products = lax.dot_general(piece, group[...].reshape(4 * rows, dim), NT, preferred_element_type=jnp.float32)
+        return jnp.min(sq - 2.0 * products, axis=0, keepdims=True)
 
     best = nearest(ce)
     emb_f = emb_ref[...].astype(jnp.float32)
@@ -195,20 +229,22 @@
 
     def one_block(gap, best):
         block = lax.rem(ce + gap, n_cent)
-        for i in range(1, chips):
-            j = lax.rem(chip + i, chips)
-            arrive(pieces.at[block, j], p_recv.at[block, j]).wait()
-        found = nearest(block)
-        return jnp.minimum(best[0], found[0]), jnp.minimum(best[1], found[1])
+        for i in range(1, span):
+            j = lax.rem(y + i, span)
+            arrive(pieces.at[block, j], y_recv.at[block, j]).wait()
+        return jnp.minimum(best, nearest(block))
 
     best = lax.fori_loop(1, n_cent, one_block, best)
 
-    min_out[...] = jnp.broadcast_to(best[1], min_out.shape)
-    min_copy = pltpu.make_async_remote_copy(
-        src_ref=min_out, dst_ref=min_in, send_sem=m_send, recv_sem=m_recv,
-        device_id=(mate, ce), device_id_type=MESH,
-    )
-    min_copy.start()
+    def min_copy(n):
+        return pltpu.make_async_remote_copy(
+            src_ref=min_out.at[n], dst_ref=min_in.at[n], send_sem=m_send.at[n], recv_sem=m_recv.at[n],
+            device_id=((mate, beside, across)[n], ce), device_id_type=MESH,
+        )
+
+    for n in range(3):
+        min_out[n] = jnp.broadcast_to(best[:, n * rows:(n + 1) * rows], min_out.shape[1:])
+        min_copy(n).start()
 
     for i in range(1, n_dp):
         other = lax.rem(dp + i, n_dp)
@@ -238,12 +274,15 @@
     member_tb = member_t.astype(jnp.bfloat16)
     counts = jnp.sum(member_t, axis=1, keepdims=True)
     in_bin = lax.broadcasted_iota(jnp.int32, (slots, NBINS), 1) == bin_col
-    own_rows = pieces[ce, chip]
+    own_rows = pieces[ce, y]
     own_f = own_rows.astype(jnp.float32)
     own_spread = jnp.dot(member_b, own_rows, preferred_element_type=jnp.float32)
 
-    min_copy.wait()
-    quant_ref[...] = (jnp.minimum(best[0], min_in[0:1]) + row_sq) * (1.0 / dim)
+    least = best[:, 3 * rows:]
+    for n in range(3):
+        min_copy(n).wait()
+        least = jnp.minimum(least, min_in[n, 0:1])
+    quant_ref[...] = (least + row_sq) * (1.0 / dim)
 
     def wait_rows(i, _):
         other = lax.rem(me + i, owners)
@@ -264,12 +303,22 @@
         spread = spread - part.astype(jnp.float32)
     hist_ref[...] = hist
 
-    mate_copy.wait_send()
+    group_copy(3, 1, beside).wait_send()
+    group_copy(3, 0, mate).wait_send()
+    group_copy(1, 2, mate).wait_send()
+
+    @pl.when(ce + 1 < n_cent)
+    def _():
+        lax.fori_loop(0, ce + 1, lambda b, _: (z_copy(b, 1, up_send).wait_send(), 0)[1], 0)
+
+    @pl.when(ce > 0)
+    def _():
+        lax.fori_loop(ce, n_cent, lambda b, _: (z_copy(b, -1, down_send).wait_send(), 0)[1], 0)
+
     for i in order:
-        z_copy(i).wait_send()
         code_copy(i).wait_send()
-        for k in range(1, chips):
-            plane_copy(k, lax.rem(ce + i, n_cent)).wait_send()
+        for k in range(1, span):
+            y_copy(k, lax.rem(ce + i, n_cent)).wait_send()
     for i in range(1, n_dp):
         spread_copy(i).wait_send()
 
@@ -283,7 +332,7 @@
 def per_device_kernel(embeddings, centroids, assign, bins):
     rows, dim = embeddings.shape
     n_dp, n_cent = lax.axis_size("dp"), lax.axis_size("cent")
-    owners, chips = n_dp * n_cent, n_dp // 2
+    owners, span = n_dp * n_cent, n_dp // 4
     cap = 2 * rows // owners
     lists = centroids.shape[0] // n_dp
     dma = pltpu.SemaphoreType.DMA
@@ -300,22 +349,21 @@
         scratch_shapes=[
             pltpu.VMEM((1, rows), jnp.int32),
             pltpu.VMEM((1, rows), jnp.int32),
-            pltpu.VMEM((rows, dim), jnp.bfloat16),
+            pltpu.VMEM((4, rows, dim), jnp.bfloat16),
             pltpu.VMEM((owners, cap, dim), jnp.bfloat16),
             pltpu.VMEM((owners, cap, dim), jnp.bfloat16),
-            pltpu.VMEM((rows, dim), jnp.bfloat16),
-            pltpu.VMEM((n_cent, chips, lists, dim), jnp.bfloat16),
-            pltpu.VMEM((8, rows), jnp.float32),
-            pltpu.VMEM((8, rows), jnp.float32),
+            pltpu.VMEM((n_cent, span, lists, dim), jnp.bfloat16),
+            pltpu.VMEM((3, 8, rows), jnp.float32),
+            pltpu.VMEM((3, 8, rows), jnp.float32),
             pltpu.VMEM((n_cent, 1, n_dp * cap), jnp.int32),
             pltpu.VMEM((n_cent, 1, n_dp * cap), jnp.int32),
             pltpu.VMEM((n_dp, n_cent, 1, n_dp * cap), jnp.int32),
-            dma((3,)), dma((chips,)),
+            dma((3,)), dma((span,)),
             dma((owners,)), dma((owners,)),
-            dma, dma,
-            dma((n_cent,)), dma((n_cent,)),
-            dma((n_cent, chips)), dma((n_cent, chips)),
-            dma, dma,
+            dma((3,)), dma((3,)),
+            dma((n_cent,)), dma((n_cent,)), dma((n_cent,)),
+            dma((n_cent, span)), dma((n_cent, span)),
+            dma((3,)), dma((3,)),
             dma((n_cent,)), dma((n_cent,)),
             dma((n_dp,)), dma((n_dp,)),
         ],
@@ -383,7 +431,7 @@
 def per_device(embeddings, centroids, assign, bins):
     n_dp = lax.axis_size("dp")
     cap = 2 * embeddings.shape[0] // (n_dp * lax.axis_size("cent"))
-    if cap % 16 == 0 and n_dp * cap % 128 == 0:
+    if cap % 16 == 0 and n_dp * cap % 128 == 0 and n_dp % 4 == 0:
         return per_device_kernel(embeddings, centroids, assign, bins)
     return per_device_plain(embeddings, centroids, assign, bins)
 

time: 43.5 us -> 39.6 us (0.910)
  the two profiles are of different devices: /device:TPU:11 before, /device:TPU:27 now
where the time goes in v3:
time: 39.6 us; the launch traced here: 39.4 us
  Pallas kernels  35.3 us (89%)
  local copies, waits for them, and re-layouts  3.51 us (9%)
  between operations  0.65 us (2%)
    pallas_call x1, Pallas kernels, per_device_kernel(): pl.pallas_call(functools.partial(kernel, n_dp, n_cent, cap), out_shape=(j...  35.3 us
    unnamed x7, local copies, waits for them, and re-layouts  3.51 us

profile of v3, /device:TPU:27, one launch (start us, length us, event | category | flops | bytes accessed | tf_op | source)
XLA Modules:
  0.0 39.4 jit_solution(13853284907911323839)
XLA Ops:
  0.6 35.3 %shard_map.67 = (f32[1,256]{1,0:T(1,128)}, f32[64,768]{1,0:T(8,128)}, f32[64,256]{1,0:T(8,128)}) custom-call(bf16[256,768]{1,0:T(8,128)(2,1)} %emb_hbm.1, bf16[512,768]{1,0:T(8,128)(2,1)} %cent_hbm.1, s32[1,256]{1,0:T(1,128)} %bitcast.4, s32[1,256]{1,0:T(1,128)} %bitcast.5), custom_call_target="tpu_custom_call" | custom-call | flops 805306368 | bytes 1572864 | tf_op jit(solution)/shard_map/pallas_call | solution.py:340
  35.9 0.0 copy-start.1
  35.9 0.7 %copy-done.1 = f32[1,256]{1,0:T(1,128)S(1)} copy-done((f32[1,256]{1,0:T(1,128)S(1)}, f32[1,256]{1,0:T(1,128)}, u32[]{:S(2)}) %copy-start.1) | copy-done | bytes 1048
  36.6 0.6 %copy.10 = f32[256]{0:T(256)} copy(f32[256]{0:T(256)S(1)} %bitcast.3) | data formatting | bytes 2048
  37.1 0.0 copy-start
  37.1 1.6 %copy.11 = f32[64,768]{1,0:T(8,128)} copy(f32[64,768]{1,0:T(8,128)} %get-tuple-element.13) | data formatting | bytes 393216
  38.8 0.0 copy-done
  38.8 0.6 %copy.12 = f32[64,256]{1,0:T(8,128)} copy(f32[64,256]{1,0:T(8,128)S(1)} %copy-done) | data formatting | bytes 131072
Async XLA Ops:
  35.9 0.7 %copy-start.1 = (f32[1,256]{1,0:T(1,128)S(1)}, f32[1,256]{1,0:T(1,128)}, u32[]{:S(2)}) copy-start(f32[1,256]{1,0:T(1,128)} %get-tuple-element.6) | copy-start | bytes 3076
  37.1 1.7 %copy-start = (f32[64,256]{1,0:T(8,128)S(1)}, f32[64,256]{1,0:T(8,128)}, u32[]{:S(2)}) copy-start(f32[64,256]{1,0:T(8,128)} %get-tuple-element.14) | copy-start | bytes 196612
